TPU v7x, 32 devices: a whole 2x2x4 slice. The times are simulated.
32 devices in a mesh: dp: 4 (over z), mp: 8 (over y, x, core).
Axes of the slice: x: 2, y: 2, z: 4, core: 2. Of those that a mesh axis runs over, the one named last changes fastest.
Arguments:
- tokens: bfloat16 [128, 4096], P(('dp', 'mp')), may hold values from -6 to 6
- hidden_grad: bfloat16 [128, 14336], P('dp', 'mp'), may hold values from -0.5 to 0.5
- gate_weight: bfloat16 [4096, 14336], P('dp', 'mp'), may hold values from -0.09375 to 0.09375
- up_weight: bfloat16 [4096, 14336], P('dp', 'mp'), may hold values from -0.09375 to 0.09375
- gate_probe: bfloat16 [4096, 14336], P('dp', 'mp'), may hold values from -1 to 1, as said below
- gate_mean: float32 [4096, 14336], P('dp', 'mp'), may hold values from -0.6 to 0.6
- gate_curve: float32 [4096, 14336], P('dp', 'mp'), may hold values from 1 to 10
- group_counts: int32 [4], replicated, may hold values from 8 to 32, as said below
Outputs:
- gate_weight_new: bfloat16 [4096, 14336], P('dp', 'mp')
- gate_mean_new: float32 [4096, 14336], P('dp', 'mp')
- gate_curve_new: float32 [4096, 14336], P('dp', 'mp')
Inputs may be any that keep to these rules, and one draw needn't show every extreme that they name: `group_counts`: some data group has exactly 32 live tokens in every draw. `gate_probe`: every entry is -1 or 1, each sign drawn independently.
All inputs are finite; a program needn't handle non-finite values.
Results may differ from a plain program's by a relative error of at most 0.0017.
Values may be sent and summed in bfloat16 or wider, within the bound.
A program may use at most 128 MiB of HBM per device.

v0:
```python
import jax
import jax.numpy as jnp
from jax import lax
from jax.sharding import PartitionSpec as P

first_decay = 0.9
second_decay = 0.999
learn_rate = 0.15
epsilon_term = 0.0001
first_fix = 1.0 - 0.9**10
second_fix = 1.0 - 0.999**10


def silu_parts(inputs):
    sigmoid_part = jax.nn.sigmoid(inputs)
    silu_slope = sigmoid_part * (1.0 + inputs * (1.0 - sigmoid_part))
    silu_bend = sigmoid_part * (1.0 - sigmoid_part) * (2.0 + inputs * (1.0 - 2.0 * sigmoid_part))
    return (silu_slope, silu_bend)


def adahessian(weight, mean_old, curve_old, gradient, probe_value, product):
    diagonal = probe_value.astype(jnp.float32) * product
    mean_new = first_decay * mean_old + (1.0 - first_decay) * gradient
    curve_new = second_decay * curve_old + (1.0 - second_decay) * diagonal * diagonal
    step_ratio = mean_new / first_fix / (jnp.sqrt(curve_new / second_fix) + epsilon_term)
    weight_new = (weight.astype(jnp.float32) - learn_rate * step_ratio).astype(jnp.bfloat16)
    return (weight_new, mean_new, curve_new)


def body(
    tokens, hidden_grad, gate_weight, up_weight, gate_probe, gate_mean, gate_curve, group_counts
):
    whole = lax.all_gather(tokens, "mp", axis=0, tiled=True)
    columns = lax.all_to_all(whole, "dp", split_axis=1, concat_axis=0, tiled=True)
    group_rows = whole.shape[0]
    width = gate_weight.shape[1]
    pieces = (
        lax.all_gather(gate_weight, "dp", axis=0, tiled=True),
        lax.all_gather(up_weight, "dp", axis=0, tiled=True),
    )
    gate_pre, up_pre = tuple(
        (jnp.dot(whole, piece, preferred_element_type=jnp.float32) for piece in pieces)
    )
    selected = columns
    gate_tan = lax.psum_scatter(
        jnp.dot(selected, gate_probe, preferred_element_type=jnp.float32),
        "dp",
        scatter_dimension=0,
        tiled=True,
    )
    group_index = lax.axis_index("dp")
    limit = lax.dynamic_index_in_dim(group_counts, group_index, 0, keepdims=False)
    live = (jnp.arange(group_rows, dtype=jnp.int32) < limit).astype(jnp.float32)
    silu_slope, silu_bend = silu_parts(gate_pre)
    masked = hidden_grad.astype(jnp.float32) * live[:, None]
    grad_gate = (masked * up_pre * silu_slope).astype(jnp.bfloat16)
    tan_gate = (masked * up_pre * silu_bend * gate_tan).astype(jnp.bfloat16)
    packed = jnp.concatenate([grad_gate, tan_gate], 1)
    selected = columns
    sums = lax.dot_general(
        selected,
        lax.all_gather(packed, "dp", axis=0, tiled=True),
        (((0,), (0,)), ((), ())),
        preferred_element_type=jnp.float32,
    )
    gate_out = adahessian(
        gate_weight, gate_mean, gate_curve, sums[:, :width], gate_probe, sums[:, width:]
    )
    return (gate_out[0], gate_out[1], gate_out[2])


def solution(mesh):
    return jax.shard_map(
        body,
        mesh=mesh,
        in_specs=(
            P(("dp", "mp"), None),
            P("dp", "mp"),
            P("dp", "mp"),
            P("dp", "mp"),
            P("dp", "mp"),
            P("dp", "mp"),
            P("dp", "mp"),
            P(),
        ),
        out_specs=(P("dp", "mp"), P("dp", "mp"), P("dp", "mp")),
        check_vma=False,
    )
```

profile of v0, /device:TPU:0, one launch (start us, length us, event | category | flops | bytes accessed | tf_op | source)
XLA Modules:
  0.0 633.7 jit_solution(5893498349573498156)
XLA Ops:
  7.2 0.0 all-gather.6.cloned.1.call-start
  7.2 0.7 all-gather.6.cloned.1.call-update
  7.9 0.0 reduce-scatter.2.cloned.1.call-start
  7.9 11.0 %all-gather = bf16[8,4,4096]{2,1,0:T(4,128)(2,1)S(1)} all-gather(bf16[1,4,4096]{2,1,0:T(4,128)(2,1)} %bitcast.17), channel_id=1, replica_groups=mesh['dp'=4,'mp'=8] {'mp'}, dimensions={0}, use_global_device_ids=true | all-gather | bytes 294912 | tf_op jit(solution)/shard_map/all_gather | solution.py:33
  18.9 0.2 all_to_all.14
  19.1 0.1 copy.35
  19.2 26.7 %all_to_all.19 = bf16[32,4,1024]{2,0,1:T(8,128)(2,1)S(1)} all-to-all(bf16[32,4,1024]{2,0,1:T(8,128)(2,1)S(1)} %copy.35), channel_id=1, replica_groups=mesh['dp'=4,'mp'=8] {'dp'}, dimensions={1} | all-to-all | bytes 524288 | tf_op jit(solution)/shard_map/all_to_all | solution.py:34
  46.0 3.6 fusion.13
  49.6 0.0 reduce-scatter.2.cloned.1.call-update
  49.6 0.0 all-gather.4.cloned.1.call-start
  49.7 0.7 all-gather.4.cloned.1.call-update
  50.4 0.1 reshape.15
  50.4 5.9 copy.33
  56.4 5.9 copy.37
  62.3 8.4 %copy.34 = f32[1024,1792]{0,1:T(8,128)} copy(f32[1024,1792]{1,0:T(8,128)} %param.13) | data formatting | bytes 14680064 | tf_op args[5]
  70.7 0.0 copy-start.1
  70.7 8.4 %copy.36 = f32[1024,1792]{0,1:T(8,128)} copy(f32[1024,1792]{1,0:T(8,128)} %param.14) | data formatting | bytes 14680064 | tf_op args[6]
  79.1 0.0 copy-done.1
  79.1 0.6 dynamic_slice.4
  79.7 0.6 compare_convert_fusion
  80.3 0.0 copy-start
  80.3 189.7 %all-gather.6.cloned.1.call-done = bf16[4096,1792]{1,0:T(8,128)(2,1)} async-done(((bf16[1024,1792]{1,0:T(8,128)(2,1)}), bf16[4096,1792]{1,0:T(8,128)(2,1)}) %all-gather.6.cloned.1.call-update) | async-done | bytes 14680080 | tf_op jit(solution)/shard_map/all_gather | solution.py:38
  270.0 7.7 %fusion.12 = f32[32,1792]{1,0:T(8,128)S(1)} fusion(bf16[32,4096]{1,0:T(8,128)(2,1)S(1)} %reshape.15, bf16[4096,1792]{1,0:T(8,128)(2,1)} %all-gather.6.cloned.1.call-done), kind=kOutput, calls=%fused_computation.21 | convolution fusion | flops 469762048 | bytes 15171584 | tf_op jit(solution)/shard_map/dot_general | solution.py:42
  277.7 17.9 %reduce-scatter.2.cloned.1.call-done = f32[32,1792]{1,0:T(8,128)} async-done(((f32[128,1792]{1,0:T(8,128)}), f32[32,1792]{1,0:T(8,128)}) %reduce-scatter.2.cloned.1.call-update) | async-done | bytes 229392 | tf_op jit(solution)/shard_map/reduce_scatter | solution.py:45
  295.6 253.0 %all-gather.4.cloned.1.call-done = bf16[4096,1792]{1,0:T(8,128)(2,1)} async-done(((bf16[1024,1792]{1,0:T(8,128)(2,1)}), bf16[4096,1792]{1,0:T(8,128)(2,1)}) %all-gather.4.cloned.1.call-update) | async-done | bytes 14680080 | tf_op jit(solution)/shard_map/all_gather | solution.py:39
  548.6 0.0 copy-done
  548.6 7.8 %fusion.5 = (bf16[32,1792]{1,0:T(8,128)(2,1)S(1)}, bf16[32,1792]{1,0:T(8,128)(2,1)S(1)}) fusion(f32[32,1792]{1,0:T(8,128)S(1)} %fusion.12, f32[32,1792]{1,0:T(8,128)} %reduce-scatter.2.cloned.1.call-done, bf16[32,4096]{1,0:T(8,128)(2,1)S(1)} %reshape.15, bf16[4096,1792]{1,0:T(8,128)(2,1)} %all-gather.4.cloned.1.call-done, f32[32]{0:T(128)S(1)} %compare_convert_fusion, ...), kind=kOutput, calls=%fused_computation.13 | convolution fusion | flops 470966272 | bytes 15745152 | tf_op jit(solution)/shard_map/dot_general | solution.py:42
  556.4 19.7 %all_gather.15 = bf16[128,3584]{1,0:T(8,128)(2,1)S(1)} all-gather(bf16[32,3584]{1,0:T(8,128)(2,1)S(1)} %pad_maximum_fusion), channel_id=1, replica_groups=mesh['dp'=4,'mp'=8] {'dp'}, dimensions={0}, use_global_device_ids=true | all-gather | bytes 1146880 | tf_op jit(solution)/shard_map/all_gather | solution.py:62
  576.1 7.3 %convolution_bitcast_fusion = f32[1024,3584]{0,1:T(8,128)} fusion(bf16[128,3584]{1,0:T(8,128)(2,1)S(1)} %all_gather.15, bf16[128,1024]{1,0:T(8,128)(2,1)S(1)} %bitcast.16), kind=kOutput, calls=%fused_computation.1 | convolution fusion | flops 939524096 | bytes 15859712 | tf_op jit(solution)/shard_map/dot_general | solution.py:60
  583.4 21.1 %subtract_convert_fusion = (bf16[1024,1792]{0,1:T(8,128)(2,1)}, f32[1024,1792]{0,1:T(8,128)}, f32[1024,1792]{0,1:T(8,128)}) fusion(bf16[1024,1792]{0,1:T(8,128)(2,1)} %copy.33, f32[1024,3584]{0,1:T(8,128)} %convolution_bitcast_fusion, f32[1024,1792]{0,1:T(8,128)} %copy.34, bf16[1024,1792]{0,1:T(8,128)(2,1)} %copy.37, f32[1024,1792]{0,1:T(8,128)} %copy.36), kind=kLoop, calls=%fused_computation.6 | loop fusion | flops 31195136 | bytes 55050240 | tf_op jit(solution)/shard_map/convert_element_type | solution.py:26
  604.6 8.4 %copy.39 = f32[1024,1792]{1,0:T(8,128)} copy(f32[1024,1792]{0,1:T(8,128)} %get-tuple-element.16) | data formatting | bytes 14680064
  612.9 8.4 %copy.40 = f32[1024,1792]{1,0:T(8,128)} copy(f32[1024,1792]{0,1:T(8,128)} %get-tuple-element.17) | data formatting | bytes 14680064
  621.3 5.9 copy.38
  (1 shorter events, 0.0 us)
Async XLA Ops:
  7.2 262.8 %all-gather.6.cloned.1.call-start = ((), (), s32[]{:S(2)}) async-start(), calls=%async_computation.3 | async-start | bytes 18350080 | tf_op jit(solution)/shard_map/all_gather | solution.py:38
  7.9 287.7 %reduce-scatter.2.cloned.1.call-start = ((), (), s32[]{:S(2)}) async-start(), calls=%async_computation.4 | async-start | bytes 1146880 | tf_op jit(solution)/shard_map/reduce_scatter | solution.py:45
  49.6 499.0 %all-gather.4.cloned.1.call-start = ((), (), s32[]{:S(2)}) async-start(), calls=%async_computation.2 | async-start | bytes 18350080 | tf_op jit(solution)/shard_map/all_gather | solution.py:39
  70.7 8.4 %copy-start.1 = (s32[4]{0:T(128)S(1)}, s32[4]{0:T(128)}, u32[]{:S(2)}) copy-start(s32[4]{0:T(128)} %param.15) | copy-start | bytes 52
  80.3 468.3 %copy-start = (bf16[32,1792]{1,0:T(8,128)(2,1)S(1)}, bf16[32,1792]{1,0:T(8,128)(2,1)}, u32[]{:S(2)}) copy-start(bf16[32,1792]{1,0:T(8,128)(2,1)} %param.9) | copy-start | bytes 344068
Sparse Core Ops, SparseCore 0:
  9.6 260.3 all-gather.5
  272.3 23.2 reduce-scatter.1
  297.1 251.4 all-gather.3
where the time goes:
time: 635 us; the launch traced here: 634 us
  waiting for transfers between devices  462 us (73%)
  blocking collectives  57.4 us (9%)
  local copies, waits for them, and re-layouts  52.3 us (8%)
  matrix products  26.4 us (4%)
  other arithmetic  21.8 us (3%)
  between operations  13.8 us (2%)
    all_gather x1, waiting for transfers between devices, body(): lax.all_gather(up_weight, 'dp', axis=0, tiled=True)  253 us
    all_gather x1, waiting for transfers between devices, body(): lax.all_gather(gate_weight, 'dp', axis=0, tiled=True)  190 us
    unnamed x12, local copies, waits for them, and re-layouts  51.4 us
    all_to_all x1, blocking collectives, body(): lax.all_to_all(whole, 'dp', split_axis=1, concat_axis=0, tiled=True)  26.7 us
    convert_element_type x1, other arithmetic, adahessian(): (weight.astype(jnp.float32) - learn_rate * step_ratio).astype(jnp.bfloat16)  21.1 us
    all_gather x1, blocking collectives, body(): lax.all_gather(packed, 'dp', axis=0, tiled=True)  19.7 us
    reduce_scatter x1, waiting for transfers between devices, body(): lax.psum_scatter(jnp.dot(selected, gate_probe, preferred_element_type=jnp...  17.9 us
    dot_general x2, matrix products, body(): jnp.dot(whole, piece, preferred_element_type=jnp.float32)  15.5 us
  transfers between devices with their start and end apart: 3, of which 3 were waited for; matrix products, arithmetic and copies ran while one was open for 7% of the time, Pallas kernels for 0%

commit v1 on v0

--- a/solution.py
+++ b/solution.py
@@ -30,24 +30,25 @@
 def body(
     tokens, hidden_grad, gate_weight, up_weight, gate_probe, gate_mean, gate_curve, group_counts
 ):
-    whole = lax.all_gather(tokens, "mp", axis=0, tiled=True)
-    columns = lax.all_to_all(whole, "dp", split_axis=1, concat_axis=0, tiled=True)
-    group_rows = whole.shape[0]
+    shards = lax.axis_size("dp")
+    local_rows, features = tokens.shape
+    own = lax.all_to_all(tokens, "dp", split_axis=1, concat_axis=0, tiled=True)
+    spread = lax.all_gather(own, "mp", axis=0)
+    peers = spread.shape[0]
+    depth = features // shards
+    columns = spread.reshape(peers, shards, local_rows, depth)
+    columns = columns.transpose(1, 0, 2, 3).reshape(-1, depth)
+    group_rows = peers * local_rows
     width = gate_weight.shape[1]
-    pieces = (
-        lax.all_gather(gate_weight, "dp", axis=0, tiled=True),
-        lax.all_gather(up_weight, "dp", axis=0, tiled=True),
+    partial = jnp.concatenate(
+        [
+            jnp.dot(columns, piece, preferred_element_type=jnp.float32)
+            for piece in (gate_weight, up_weight, gate_probe)
+        ],
+        axis=1,
     )
-    gate_pre, up_pre = tuple(
-        (jnp.dot(whole, piece, preferred_element_type=jnp.float32) for piece in pieces)
-    )
-    selected = columns
-    gate_tan = lax.psum_scatter(
-        jnp.dot(selected, gate_probe, preferred_element_type=jnp.float32),
-        "dp",
-        scatter_dimension=0,
-        tiled=True,
-    )
+    total = lax.psum_scatter(partial, "dp", scatter_dimension=0, tiled=True)
+    gate_pre, up_pre, gate_tan = (total[:, i * width : (i + 1) * width] for i in range(3))
     group_index = lax.axis_index("dp")
     limit = lax.dynamic_index_in_dim(group_counts, group_index, 0, keepdims=False)
     live = (jnp.arange(group_rows, dtype=jnp.int32) < limit).astype(jnp.float32)
@@ -56,17 +57,15 @@
     grad_gate = (masked * up_pre * silu_slope).astype(jnp.bfloat16)
     tan_gate = (masked * up_pre * silu_bend * gate_tan).astype(jnp.bfloat16)
     packed = jnp.concatenate([grad_gate, tan_gate], 1)
-    selected = columns
     sums = lax.dot_general(
-        selected,
+        columns,
         lax.all_gather(packed, "dp", axis=0, tiled=True),
         (((0,), (0,)), ((), ())),
         preferred_element_type=jnp.float32,
     )
-    gate_out = adahessian(
+    return adahessian(
         gate_weight, gate_mean, gate_curve, sums[:, :width], gate_probe, sums[:, width:]
     )
-    return (gate_out[0], gate_out[1], gate_out[2])
 
 
 def solution(mesh):

time: 635 us -> 168 us (0.26)
  waiting for transfers between devices: 462 us -> 21.8 us
  blocking collectives: 57.4 us -> 40.8 us
  matrix products: 26.4 us -> 13.5 us
    all_gather x2 -> x0, waiting for transfers between devices: 443 us -> none  [the longest x1 253 us: body(): lax.all_gather(up_weight, 'dp', axis=0, tiled=True)]
    all_to_all x1, blocking collectives: 26.7 us -> 12 us  [body(): own = lax.all_to_all(tokens, 'dp', split_axis=1, concat_axis=0, tiled=True)]
    dot_general x4, matrix products: 26.4 us -> 13.5 us  [the longest x1 7.3 us: body(): lax.dot_general(columns, lax.all_gather(packed, 'dp', axis=0, tiled=True)...]
    unnamed x12 -> x13, local copies, waits for them, and re-layouts: 51.4 us -> 51.5 us
  transfers between devices with their start and end apart: 3 -> 1, of which waited for: 3 -> 1; matrix products, arithmetic and copies ran while one was open for 7% -> 18% of each run, Pallas kernels for 0% -> 0%
where the time goes in v1:
time: 168 us; the launch traced here: 167 us
  local copies, waits for them, and re-layouts  52.3 us (31%)
  blocking collectives  40.8 us (24%)
  other arithmetic  24.9 us (15%)
  waiting for transfers between devices  21.8 us (13%)
  between operations  14.1 us (8%)
  matrix products  13.5 us (8%)
    unnamed x13, local copies, waits for them, and re-layouts  51.5 us
    reduce_scatter x1, waiting for transfers between devices, body(): total = lax.psum_scatter(partial, 'dp', scatter_dimension=0, tiled=True)  21.8 us
    convert_element_type x1, other arithmetic, adahessian(): (weight.astype(jnp.float32) - learn_rate * step_ratio).astype(jnp.bfloat16)  21.2 us
    all_gather x1, blocking collectives, body(): lax.all_gather(packed, 'dp', axis=0, tiled=True)  19.5 us
    all_to_all x1, blocking collectives, body(): own = lax.all_to_all(tokens, 'dp', split_axis=1, concat_axis=0, tiled=True)  12 us
    all_gather x1, blocking collectives, body(): spread = lax.all_gather(own, 'mp', axis=0)  9.32 us
    dot_general x1, matrix products, body(): lax.dot_general(columns, lax.all_gather(packed, 'dp', axis=0, tiled=True)...  7.3 us
    dot_general x3, matrix products, body(): jnp.dot(columns, piece, preferred_element_type=jnp.float32)  6.17 us
  transfers between devices with their start and end apart: 1, of which 1 were waited for; matrix products, arithmetic and copies ran while one was open for 18% of the time, Pallas kernels for 0%

profile of v1, /device:TPU:0, one launch (start us, length us, event | category | flops | bytes accessed | tf_op | source)
XLA Modules:
  0.0 167.4 jit_solution(15452338479708502730)
XLA Ops:
  7.2 0.0 reduce-scatter.2.cloned.1.call-start
  7.2 12.0 %all_to_all.16 = bf16[4,4,1024]{2,0,1:T(4,128)(2,1)S(1)} all-to-all(bf16[4,4,1024]{2,0,1:T(4,128)(2,1)} %bitcast.18), channel_id=1, replica_groups=mesh['dp'=4,'mp'=8] {'dp'}, dimensions={1} | all-to-all | bytes 65536 | tf_op jit(solution)/shard_map/all_to_all | solution.py:35
  19.2 9.3 %all_gather.10 = bf16[8,16,1024]{2,1,0:T(8,128)(2,1)S(1)} all-gather(bf16[1,16,1024]{2,1,0:T(8,128)(2,1)S(1)} %all_gather.9), channel_id=1, replica_groups=mesh['dp'=4,'mp'=8] {'mp'}, dimensions={0}, use_global_device_ids=true | all-gather | bytes 294912 | tf_op jit(solution)/shard_map/all_gather | solution.py:36
  28.5 0.1 reshape.21
  28.6 0.1 copy.37
  28.7 0.1 reshape.22
  28.8 0.0 copy-start
  28.8 2.8 %fusion.12 = f32[128,1792]{1,0:T(8,128)S(1)} fusion(bf16[128,1024]{1,0:T(8,128)(2,1)S(1)} %reshape.22, bf16[1024,1792]{1,0:T(8,128)(2,1)} %param.10), kind=kOutput, calls=%fused_computation.23 | convolution fusion | flops 469762048 | bytes 4849664 | tf_op jit(solution)/shard_map/dot_general | solution.py:45
  31.7 2.7 %fusion.13 = f32[128,1792]{1,0:T(8,128)S(1)} fusion(bf16[128,1024]{1,0:T(8,128)(2,1)S(1)} %reshape.22, bf16[1024,1792]{1,0:T(8,128)(2,1)} %param.11), kind=kOutput, calls=%fused_computation.24 | convolution fusion | flops 469762048 | bytes 4849664 | tf_op jit(solution)/shard_map/dot_general | solution.py:45
  34.4 0.0 copy-done
  34.4 0.6 fusion.14
  35.0 1.7 %pad_maximum_fusion = f32[128,5376]{1,0:T(8,128)} fusion(f32[128,1792]{1,0:T(8,128)S(1)} %fusion.14, f32[128,1792]{1,0:T(8,128)S(1)} %fusion.13, f32[128,1792]{1,0:T(8,128)S(1)} %fusion.12), kind=kLoop, calls=%fused_computation.7 | loop fusion | flops 1376256 | bytes 5505024 | tf_op jit(solution)/shard_map/concatenate | solution.py:43
  36.8 0.0 reduce-scatter.2.cloned.1.call-update
  36.8 6.0 %copy.27 = bf16[1024,1792]{0,1:T(8,128)(2,1)} copy(bf16[1024,1792]{1,0:T(8,128)(2,1)} %param.10) | data formatting | bytes 7340032 | tf_op args[2]
  42.8 6.0 %copy.32 = bf16[1024,1792]{0,1:T(8,128)(2,1)} copy(bf16[1024,1792]{1,0:T(8,128)(2,1)} %param.12) | data formatting | bytes 7340032 | tf_op args[4]
  48.8 8.4 %copy.28 = f32[1024,1792]{0,1:T(8,128)} copy(f32[1024,1792]{1,0:T(8,128)} %param.13) | data formatting | bytes 14680064 | tf_op args[5]
  57.1 0.0 copy-start.2
  57.1 0.0 copy-start.1
  57.1 8.5 %copy.31 = f32[1024,1792]{0,1:T(8,128)} copy(f32[1024,1792]{1,0:T(8,128)} %param.14) | data formatting | bytes 14680064 | tf_op args[6]
  65.6 0.0 copy-done.2
  65.6 0.6 dynamic_slice.4
  66.2 0.6 compare_convert_fusion
  66.8 21.8 %reduce-scatter.2.cloned.1.call-done = f32[32,5376]{1,0:T(8,128)} async-done(((f32[128,5376]{1,0:T(8,128)}), f32[32,5376]{1,0:T(8,128)}) %reduce-scatter.2.cloned.1.call-update) | async-done | bytes 688144 | tf_op jit(solution)/shard_map/reduce_scatter | solution.py:50
  88.6 0.0 copy-done.1
  88.6 1.3 fusion.5
  89.9 19.5 %all_gather.11 = bf16[128,3584]{1,0:T(8,128)(2,1)S(1)} all-gather(bf16[32,3584]{1,0:T(8,128)(2,1)S(1)} %pad_maximum_fusion.1), channel_id=1, replica_groups=mesh['dp'=4,'mp'=8] {'dp'}, dimensions={0}, use_global_device_ids=true | all-gather | bytes 1146880 | tf_op jit(solution)/shard_map/all_gather | solution.py:62
  109.4 7.3 %convolution_bitcast_fusion = f32[1024,3584]{0,1:T(8,128)} fusion(bf16[128,3584]{1,0:T(8,128)(2,1)S(1)} %all_gather.11, bf16[128,1024]{1,0:T(8,128)(2,1)S(1)} %reshape.22), kind=kOutput, calls=%fused_computation.1 | convolution fusion | flops 939524096 | bytes 15859712 | tf_op jit(solution)/shard_map/dot_general | solution.py:60
  116.7 21.2 %subtract_convert_fusion = (bf16[1024,1792]{0,1:T(8,128)(2,1)}, f32[1024,1792]{0,1:T(8,128)}, f32[1024,1792]{0,1:T(8,128)}) fusion(bf16[1024,1792]{0,1:T(8,128)(2,1)} %copy.27, f32[1024,3584]{0,1:T(8,128)} %convolution_bitcast_fusion, f32[1024,1792]{0,1:T(8,128)} %copy.28, bf16[1024,1792]{0,1:T(8,128)(2,1)} %copy.32, f32[1024,1792]{0,1:T(8,128)} %copy.31), kind=kLoop, calls=%fused_computation.6 | loop fusion | flops 31195136 | bytes 55050240 | tf_op jit(solution)/shard_map/convert_element_type | solution.py:26
  137.9 8.4 %copy.34 = f32[1024,1792]{1,0:T(8,128)} copy(f32[1024,1792]{0,1:T(8,128)} %get-tuple-element.13) | data formatting | bytes 14680064
  146.3 8.4 %copy.35 = f32[1024,1792]{1,0:T(8,128)} copy(f32[1024,1792]{0,1:T(8,128)} %get-tuple-element.14) | data formatting | bytes 14680064
  154.6 5.9 %copy.33 = bf16[1024,1792]{1,0:T(8,128)(2,1)} copy(bf16[1024,1792]{0,1:T(8,128)(2,1)} %get-tuple-element.12) | data formatting | bytes 7340032
  (2 shorter events, 0.0 us)
Async XLA Ops:
  7.2 81.4 %reduce-scatter.2.cloned.1.call-start = ((), (), s32[]{:S(2)}) async-start(), calls=%async_computation.2 | async-start | bytes 3440640 | tf_op jit(solution)/shard_map/reduce_scatter | solution.py:50
  28.8 5.6 %copy-start = (bf16[1024,1792]{1,0:T(8,128)(2,1)S(1)}, bf16[1024,1792]{1,0:T(8,128)(2,1)}, u32[]{:S(2)}) copy-start(bf16[1024,1792]{1,0:T(8,128)(2,1)} %param.12) | copy-start | bytes 11010052
  57.1 8.5 %copy-start.2 = (s32[4]{0:T(128)S(1)}, s32[4]{0:T(128)}, u32[]{:S(2)}) copy-start(s32[4]{0:T(128)} %param.15) | copy-start | bytes 52
  57.1 31.4 %copy-start.1 = (bf16[32,1792]{1,0:T(8,128)(2,1)S(1)}, bf16[32,1792]{1,0:T(8,128)(2,1)}, u32[]{:S(2)}) copy-start(bf16[32,1792]{1,0:T(8,128)(2,1)} %param.9) | copy-start | bytes 344068
Sparse Core Ops, SparseCore 0:
  36.9 51.6 reduce-scatter.1

commit v2 on v1

--- a/solution.py
+++ b/solution.py
@@ -1,6 +1,10 @@
+import functools
+
 import jax
 import jax.numpy as jnp
 from jax import lax
+from jax.experimental import pallas as pl
+from jax.experimental.pallas import tpu as pltpu
 from jax.sharding import PartitionSpec as P
 
 first_decay = 0.9
@@ -27,7 +31,7 @@
     return (weight_new, mean_new, curve_new)
 
 
-def body(
+def plain_body(
     tokens, hidden_grad, gate_weight, up_weight, gate_probe, gate_mean, gate_curve, group_counts
 ):
     shards = lax.axis_size("dp")
@@ -68,6 +72,336 @@
     )
 
 
+CHUNK = 256
+LAG = 2
+BACK = 6
+
+
+def exchange_kernel(
+    shards, peers, tok_ref, grad_ref, gate_ref, up_ref, probe_ref, g_ref, colt_ref,
+    w, s1, s2, cols, grad, pbuf, rbuf,
+    wsem, s1_send, s1_recv, s2_send, s2_recv, h_send, h_recv, p_send, p_recv, g_send, g_recv,
+):
+    d = lax.axis_index("dp")
+    m = lax.axis_index("mp")
+    last = shards - 1
+    features = tok_ref.shape[1]
+    rows = tok_ref.shape[0]
+    depth = features // shards
+    width = gate_ref.shape[1]
+    chunks = width // CHUNK
+    total = rows * peers
+    half = total // 2
+    group = grad_ref.shape[0]
+
+    loads = [
+        pltpu.make_async_copy(ref, w.at[i], wsem.at[i])
+        for i, ref in enumerate((gate_ref, up_ref, probe_ref))
+    ]
+    for load in loads:
+        load.start()
+
+    barrier = pltpu.get_barrier_semaphore()
+    for k in range(1, shards):
+        pl.semaphore_signal(
+            barrier, inc=1, device_id=(lax.rem(d + k, shards), m),
+            device_id_type=pl.DeviceIdType.MESH,
+        )
+    for k in range(1, peers):
+        pl.semaphore_signal(
+            barrier, inc=1, device_id=(d, lax.rem(m + k, peers)),
+            device_id_type=pl.DeviceIdType.MESH,
+        )
+    pl.semaphore_wait(barrier, shards + peers - 2)
+
+    def remote(src, dst, send, recv, device):
+        return pltpu.make_async_remote_copy(
+            src_ref=src, dst_ref=dst, send_sem=send, recv_sem=recv,
+            device_id=device, device_id_type=pl.DeviceIdType.MESH,
+        )
+
+    first = []
+    for k in range(1, shards):
+        to = lax.rem(d + k, shards)
+        first.append(
+            remote(
+                tok_ref.at[:, pl.ds(pl.multiple_of(to * depth, depth), depth)],
+                s1.at[k - 1], s1_send.at[k - 1], s1_recv.at[k - 1], (to, m),
+            )
+        )
+        first[-1].start()
+
+    low = remote(grad_ref, grad.at[pl.ds(group, group)], h_send, h_recv, (0, m))
+    high = remote(grad_ref, grad.at[pl.ds(0, group)], h_send, h_recv, (last, m))
+
+    @pl.when(d == 1)
+    def _():
+        low.start()
+
+    @pl.when(d == 2)
+    def _():
+        high.start()
+
+    @pl.when(d == 0)
+    def _():
+        grad[pl.ds(0, group), :] = grad_ref[...]
+
+    @pl.when(d == last)
+    def _():
+        grad[pl.ds(group, group), :] = grad_ref[...]
+
+    joined = tok_ref[:, pl.ds(pl.multiple_of(d * depth, depth), depth)].astype(jnp.float32)
+    for k in range(1, shards):
+        first[k - 1].wait_recv()
+        joined = joined + s1[k - 1].astype(jnp.float32)
+    s2[m] = joined.astype(jnp.bfloat16)
+    second = []
+    for k in range(1, peers):
+        second.append(
+            remote(
+                s2.at[m], s2.at[m], s2_send.at[k - 1], s2_recv.at[k - 1],
+                (d, lax.rem(m + k, peers)),
+            )
+        )
+        second[-1].start()
+    for copy in second:
+        copy.wait_recv()
+
+    local = rows // shards
+    target = lax.broadcasted_iota(jnp.int32, (total, total), 0)
+    source = lax.broadcasted_iota(jnp.int32, (total, total), 1)
+    t_group = target // group
+    t_rest = target - t_group * group
+    t_peer = t_rest // local
+    wanted = t_peer * rows + t_group * local + (t_rest - t_peer * local)
+    order = jnp.where(wanted == source, 1.0, 0.0).astype(jnp.bfloat16)
+    sorted_rows = jnp.dot(
+        order, s2[...].reshape(total, depth), preferred_element_type=jnp.float32
+    )
+    cols[...] = sorted_rows.astype(jnp.bfloat16)
+    colt_ref[...] = sorted_rows.T.astype(jnp.bfloat16)
+    for load in loads:
+        load.wait()
+
+    places = (last - d, d)
+    nexts = (jnp.maximum(d - 1, 0), jnp.minimum(d + 1, last))
+    prevs = (jnp.minimum(d + 1, last), jnp.maximum(d - 1, 0))
+
+    def forward(c, side):
+        return remote(
+            pbuf.at[c, side], rbuf.at[c, side], p_send.at[c, side], p_recv.at[c, side],
+            (nexts[side], m),
+        )
+
+    def backward(c, side):
+        part = g_ref.at[c, pl.ds(side * half, half)]
+        return remote(part, part, g_send.at[c, side], g_recv.at[c, side], (prevs[side], m))
+
+    def multiply(c):
+        where = pl.ds(pl.multiple_of(c * CHUNK, CHUNK), CHUNK)
+        for i in range(3):
+            product = jnp.dot(cols[...], w[i, :, where], preferred_element_type=jnp.float32)
+            for side in range(2):
+                pbuf[c, side, :, pl.ds(i * CHUNK, CHUNK)] = product[side * half : (side + 1) * half]
+        for side in range(2):
+
+            @pl.when(places[side] == 0)
+            def _():
+                forward(c, side).start()
+
+    def relay(c):
+        where = pl.ds(pl.multiple_of(c * CHUNK, CHUNK), CHUNK)
+        for side in range(2):
+
+            @pl.when(places[side] > 0)
+            def _():
+                forward(c, side).wait_recv()
+
+            @pl.when(jnp.logical_and(places[side] > 0, places[side] < last))
+            def _():
+                pbuf[c, side] = pbuf[c, side] + rbuf[c, side]
+                forward(c, side).start()
+
+            @pl.when(places[side] == last)
+            def _():
+                gate_pre, up_pre, gate_tan = (
+                    pbuf[c, side, :, pl.ds(i * CHUNK, CHUNK)]
+                    + rbuf[c, side, :, pl.ds(i * CHUNK, CHUNK)]
+                    for i in range(3)
+                )
+                silu_slope, silu_bend = silu_parts(gate_pre)
+                scaled = grad[:, where].astype(jnp.float32) * up_pre
+                g_ref[c, pl.ds(side * half, half), pl.ds(0, CHUNK)] = (
+                    scaled * silu_slope
+                ).astype(jnp.bfloat16)
+                g_ref[c, pl.ds(side * half, half), pl.ds(CHUNK, CHUNK)] = (
+                    scaled * silu_bend * gate_tan
+                ).astype(jnp.bfloat16)
+                backward(c, side).start()
+
+    def give_back(c):
+        for side in range(2):
+
+            @pl.when(places[side] < last)
+            def _():
+                backward(c, side).wait_recv()
+
+            @pl.when(jnp.logical_and(places[side] > 0, places[side] < last))
+            def _():
+                backward(c, side).start()
+
+    @pl.when(d == 0)
+    def _():
+        low.wait_recv()
+
+    @pl.when(d == last)
+    def _():
+        high.wait_recv()
+
+    def step(s, carry):
+        @pl.when(s < chunks)
+        def _():
+            multiply(s)
+
+        @pl.when(jnp.logical_and(s >= LAG, s < chunks + LAG))
+        def _():
+            relay(s - LAG)
+
+        @pl.when(s >= BACK)
+        def _():
+            give_back(s - BACK)
+
+        return carry
+
+    lax.fori_loop(0, chunks + BACK, step, 0)
+
+    def drain(c, carry):
+        for side in range(2):
+
+            @pl.when(places[side] < last)
+            def _():
+                forward(c, side).wait_send()
+
+            @pl.when(places[side] > 0)
+            def _():
+                backward(c, side).wait_send()
+
+        return carry
+
+    lax.fori_loop(0, chunks, drain, 0)
+    for copy in first + second:
+        copy.wait_send()
+
+    @pl.when(d == 1)
+    def _():
+        low.wait_send()
+
+    @pl.when(d == 2)
+    def _():
+        high.wait_send()
+
+
+def exchange(padded, grad, gate_weight, up_weight, gate_probe):
+    shards, peers = lax.axis_size("dp"), lax.axis_size("mp")
+    rows, features = padded.shape
+    depth, width = gate_weight.shape
+    chunks = width // CHUNK
+    total = rows * peers
+    half = total // 2
+    vmem = pl.BlockSpec(memory_space=pltpu.VMEM)
+    hbm = pl.BlockSpec(memory_space=pl.ANY)
+    dma = pltpu.SemaphoreType.DMA
+    return pl.pallas_call(
+        functools.partial(exchange_kernel, shards, peers),
+        out_shape=(
+            jax.ShapeDtypeStruct((chunks, total, 2 * CHUNK), jnp.bfloat16),
+            jax.ShapeDtypeStruct((depth, total), jnp.bfloat16),
+        ),
+        in_specs=[vmem, vmem, hbm, hbm, hbm],
+        out_specs=(vmem, vmem),
+        scratch_shapes=[
+            pltpu.VMEM((3, depth, width), jnp.bfloat16),
+            pltpu.VMEM((shards - 1, rows, depth), jnp.bfloat16),
+            pltpu.VMEM((peers, rows, depth), jnp.bfloat16),
+            pltpu.VMEM((total, depth), jnp.bfloat16),
+            pltpu.VMEM((half, width), jnp.bfloat16),
+            pltpu.VMEM((chunks, 2, half, 3 * CHUNK), jnp.float32),
+            pltpu.VMEM((chunks, 2, half, 3 * CHUNK), jnp.float32),
+            dma((3,)),
+            dma((shards - 1,)),
+            dma((shards - 1,)),
+            dma((peers - 1,)),
+            dma((peers - 1,)),
+            dma,
+            dma,
+            dma((chunks, 2)),
+            dma((chunks, 2)),
+            dma((chunks, 2)),
+            dma((chunks, 2)),
+        ],
+        compiler_params=pltpu.CompilerParams(
+            collective_id=0, has_side_effects=True, vmem_limit_bytes=40 << 20
+        ),
+    )(padded, grad, gate_weight, up_weight, gate_probe)
+
+
+def update_kernel(
+    colt_ref, g_ref, weight_ref, probe_ref, mean_ref, curve_ref, weight_out, mean_out, curve_out
+):
+    sums = jnp.dot(colt_ref[...], g_ref[0], preferred_element_type=jnp.float32)
+    weight_out[...], mean_out[...], curve_out[...] = adahessian(
+        weight_ref[...], mean_ref[...], curve_ref[...],
+        sums[:, :CHUNK], probe_ref[...], sums[:, CHUNK:],
+    )
+
+
+UPDATE_ROWS = 512
+
+
+def update(colt, g, weight, probe, mean, curve):
+    depth, width = weight.shape
+    total = colt.shape[1]
+    block = pl.BlockSpec((UPDATE_ROWS, CHUNK), lambda i, j: (j, i))
+    return pl.pallas_call(
+        update_kernel,
+        grid=(width // CHUNK, depth // UPDATE_ROWS),
+        in_specs=[
+            pl.BlockSpec((UPDATE_ROWS, total), lambda i, j: (j, 0)),
+            pl.BlockSpec((1, total, 2 * CHUNK), lambda i, j: (i, 0, 0)),
+            block, block, block, block,
+        ],
+        out_specs=(block, block, block),
+        out_shape=(
+            jax.ShapeDtypeStruct(weight.shape, weight.dtype),
+            jax.ShapeDtypeStruct(mean.shape, mean.dtype),
+            jax.ShapeDtypeStruct(curve.shape, curve.dtype),
+        ),
+        compiler_params=pltpu.CompilerParams(vmem_limit_bytes=32 << 20),
+    )(colt, g, weight, probe, mean, curve)
+
+
+def body(
+    tokens, hidden_grad, gate_weight, up_weight, gate_probe, gate_mean, gate_curve, group_counts
+):
+    shards = lax.axis_size("dp")
+    local, depth, width = tokens.shape[0], gate_weight.shape[0], gate_weight.shape[1]
+    fits = shards == 4 and (shards * local) % 16 == 0 and hidden_grad.shape[0] % 16 == 0
+    if not (fits and width % CHUNK == 0 and depth % UPDATE_ROWS == 0 and width <= 2048):
+        return plain_body(
+            tokens, hidden_grad, gate_weight, up_weight, gate_probe,
+            gate_mean, gate_curve, group_counts,
+        )
+    d = lax.axis_index("dp")
+    limit = lax.dynamic_index_in_dim(group_counts, d, 0, keepdims=False)
+    live = jnp.arange(hidden_grad.shape[0], dtype=jnp.int32) < limit
+    grad = jnp.where(live[:, None], hidden_grad, jnp.zeros_like(hidden_grad))
+    slot = jnp.arange(shards * local, dtype=jnp.int32) // local
+    repeated = jnp.tile(tokens, (shards, 1))
+    padded = jnp.where((slot == d)[:, None], repeated, jnp.zeros_like(repeated))
+    g, colt = exchange(padded, grad, gate_weight, up_weight, gate_probe)
+    return update(colt, g, gate_weight, gate_probe, gate_mean, gate_curve)
+
+
 def solution(mesh):
     return jax.shard_map(
         body,

time: 168 us -> 165 us (0.982)
  Pallas kernels: 0 us -> 154 us
  local copies, waits for them, and re-layouts: 52.3 us -> 8.2 us
  blocking collectives: 40.8 us -> 0 us
  other arithmetic: 24.9 us -> 1.72 us
  waiting for transfers between devices: 21.8 us -> 0 us
  matrix products: 13.5 us -> 0 us
  between operations: 14.1 us -> 0.69 us
    pallas_call x0 -> x2, Pallas kernels: none -> 154 us  [the longest x1 137 us: exchange(): pl.pallas_call(functools.partial(exchange_kernel, shards, peers), out_sha...]
    unnamed x13 -> x10, local copies, waits for them, and re-layouts: 51.5 us -> 6.12 us
    all_gather x2 -> x0, blocking collectives: 28.8 us -> none  [the longest x1 19.5 us: body(): lax.all_gather(packed, 'dp', axis=0, tiled=True)]
    convert_element_type x3 -> x0, other arithmetic: 23.1 us -> none  [the longest x1 21.2 us: adahessian(): (weight.astype(jnp.float32) - learn_rate * step_ratio).astype(jnp.bfloat16)]
    reduce_scatter x1 -> x0, waiting for transfers between devices: 21.8 us -> none  [body(): total = lax.psum_scatter(partial, 'dp', scatter_dimension=0, tiled=True)]
    dot_general x4 -> x0, matrix products: 13.5 us -> none  [the longest x1 7.3 us: body(): lax.dot_general(columns, lax.all_gather(packed, 'dp', axis=0, tiled=True)...]
    all_to_all x1 -> x0, blocking collectives: 12 us -> none  [body(): own = lax.all_to_all(tokens, 'dp', split_axis=1, concat_axis=0, tiled=True)]
    concatenate x2 -> x0, other arithmetic: 1.74 us -> none  [the longest x1 1.73 us: body(): jnp.concatenate([jnp.dot(columns, piece, preferred_element_type=jnp.float...]
  transfers between devices with their start and end apart: 1 -> 0, of which waited for: 1 -> 0; matrix products, arithmetic and copies ran while one was open for 18% -> 0% of each run, Pallas kernels for 0% -> 0%
where the time goes in v2:
time: 165 us
  Pallas kernels  154 us (93%)
  local copies, waits for them, and re-layouts  8.2 us (5%)
  other arithmetic  1.72 us (1%)
    pallas_call x1, Pallas kernels, exchange(): pl.pallas_call(functools.partial(exchange_kernel, shards, peers), out_sha...  137 us
    pallas_call x1, Pallas kernels, update(): pl.pallas_call(update_kernel, grid=(width // CHUNK, depth // UPDATE_ROWS)...  16.7 us
    unnamed x10, local copies, waits for them, and re-layouts  6.12 us

profile of v2, /device:TPU:0, one launch (start us, length us, event | category | flops | bytes accessed | tf_op | source)
XLA Modules:
  0.0 164.5 jit_solution(17211008898519306533)
XLA Ops:
  0.6 1.2 dynamic_slice.4
  1.9 0.6 iota_compare_fusion
  2.5 1.0 broadcast_select_fusion.1.grad_ref
  3.5 0.8 tile.4
  4.4 0.1 broadcast_select_fusion.tok_ref
  4.5 0.0 copy-start
  4.5 2.0 %copy-done = bf16[1024,1792]{1,0:T(8,128)(2,1)S(1)} copy-done((bf16[1024,1792]{1,0:T(8,128)(2,1)S(1)}, bf16[1024,1792]{1,0:T(8,128)(2,1)}, u32[]{:S(2)}) %copy-start) | copy-done | bytes 3670040
  6.5 0.0 copy-start.2
  6.5 2.0 %copy-done.2 = bf16[1024,1792]{1,0:T(8,128)(2,1)S(1)} copy-done((bf16[1024,1792]{1,0:T(8,128)(2,1)S(1)}, bf16[1024,1792]{1,0:T(8,128)(2,1)}, u32[]{:S(2)}) %copy-start.2) | copy-done | bytes 3670040
  8.5 0.0 copy-start.4
  8.5 2.0 %copy-done.4 = bf16[1024,1792]{1,0:T(8,128)(2,1)S(1)} copy-done((bf16[1024,1792]{1,0:T(8,128)(2,1)S(1)}, bf16[1024,1792]{1,0:T(8,128)(2,1)}, u32[]{:S(2)}) %copy-start.4) | copy-done | bytes 3670040
  10.6 0.0 copy-start.1
  10.6 0.0 copy-start.3
  10.6 137.2 %shard_map.103 = (bf16[7,128,512]{2,1,0:T(8,128)(2,1)S(1)}, bf16[1024,128]{1,0:T(8,128)(2,1)S(1)}) custom-call(bf16[16,4096]{1,0:T(8,128)(2,1)S(1)} %broadcast_select_fusion.tok_ref, bf16[32,1792]{1,0:T(8,128)(2,1)S(1)} %broadcast_select_fusion.1.grad_ref, bf16[1024,1792]{1,0:T(8,128)(2,1)S(1)} %copy-done, bf16[1024,1792]{1,0:T(8,128)(2,1)S(1)} %copy-done.4, ...), custom_call_target="tpu_custom_call" | custom-call | tf_op jit(solution)/shard_map/pallas_call | solution.py:314
  147.8 0.0 copy-done.1
  147.8 0.0 copy-done.3
  147.8 16.7 %shard_map.104 = (bf16[1024,1792]{1,0:T(8,128)(2,1)}, f32[1024,1792]{1,0:T(8,128)}, f32[1024,1792]{1,0:T(8,128)}) custom-call(bf16[1024,128]{1,0:T(8,128)(2,1)S(1)} %get-tuple-element.5.colt_ref, bf16[7,128,512]{2,1,0:T(8,128)(2,1)S(1)} %get-tuple-element.6.g_ref, bf16[1024,1792]{1,0:T(8,128)(2,1)S(1)} %copy-done.1, bf16[1024,1792]{1,0:T(8,128)(2,1)S(1)} %copy-done.2, ...), custom_call_target="tpu_custom_call" | custom-call | tf_op jit(solution)/shard_map/pallas_call | solution.py:365
  (2 shorter events, 0.0 us)
Async XLA Ops:
  4.5 2.0 %copy-start = (bf16[1024,1792]{1,0:T(8,128)(2,1)S(1)}, bf16[1024,1792]{1,0:T(8,128)(2,1)}, u32[]{:S(2)}) copy-start(bf16[1024,1792]{1,0:T(8,128)(2,1)} %weight_ref.1) | copy-start | bytes 11010052
  6.5 2.0 %copy-start.2 = (bf16[1024,1792]{1,0:T(8,128)(2,1)S(1)}, bf16[1024,1792]{1,0:T(8,128)(2,1)}, u32[]{:S(2)}) copy-start(bf16[1024,1792]{1,0:T(8,128)(2,1)} %probe_ref.3) | copy-start | bytes 11010052
  8.5 2.0 %copy-start.4 = (bf16[1024,1792]{1,0:T(8,128)(2,1)S(1)}, bf16[1024,1792]{1,0:T(8,128)(2,1)}, u32[]{:S(2)}) copy-start(bf16[1024,1792]{1,0:T(8,128)(2,1)} %up_ref.1) | copy-start | bytes 11010052
  10.6 137.2 %copy-start.1 = (bf16[1024,1792]{1,0:T(8,128)(2,1)S(1)}, bf16[1024,1792]{1,0:T(8,128)(2,1)}, u32[]{:S(2)}) copy-start(bf16[1024,1792]{1,0:T(8,128)(2,1)} %weight_ref.1) | copy-start | bytes 11010052
  10.6 137.2 %copy-start.3 = (f32[1024,1792]{1,0:T(8,128)S(1)}, f32[1024,1792]{1,0:T(8,128)}, u32[]{:S(2)}) copy-start(f32[1024,1792]{1,0:T(8,128)} %mean_ref.1) | copy-start | bytes 22020100

commit v3 on v2

--- a/solution.py
+++ b/solution.py
@@ -72,9 +72,9 @@
     )
 
 
-CHUNK = 256
-LAG = 2
-BACK = 6
+CHUNK = 128
+FLIGHT = 1
+GROUPED = 2
 
 
 def exchange_kernel(
@@ -205,50 +205,69 @@
                 pbuf[c, side, :, pl.ds(i * CHUNK, CHUNK)] = product[side * half : (side + 1) * half]
         for side in range(2):
 
+            @pl.when(jnp.logical_and(places[side] == 0, c >= FLIGHT))
+            def _():
+                forward(c - FLIGHT, side).wait_send()
+
             @pl.when(places[side] == 0)
             def _():
                 forward(c, side).start()
 
-    def relay(c):
+    def relay(s):
+        for side in range(2):
+            c = s - places[side]
+            inside = jnp.logical_and(c >= 0, c < chunks)
+
+            @pl.when(inside)
+            def _(c=c, side=side):
+                relay_side(c, side)
+
+    def relay_side(c, side):
         where = pl.ds(pl.multiple_of(c * CHUNK, CHUNK), CHUNK)
+
+        @pl.when(places[side] > 0)
+        def _():
+            forward(c, side).wait_recv()
+
+        @pl.when(jnp.logical_and(places[side] > 0, places[side] < last))
+        def _():
+            pbuf[c, side] = pbuf[c, side] + rbuf[c, side]
+            forward(c, side).start()
+
+        @pl.when(places[side] == last)
+        def _():
+            gate_pre, up_pre, gate_tan = (
+                pbuf[c, side, :, pl.ds(i * CHUNK, CHUNK)]
+                + rbuf[c, side, :, pl.ds(i * CHUNK, CHUNK)]
+                for i in range(3)
+            )
+            silu_slope, silu_bend = silu_parts(gate_pre)
+            scaled = grad[:, where].astype(jnp.float32) * up_pre
+            g_ref[c, pl.ds(side * half, half), pl.ds(0, CHUNK)] = (
+                scaled * silu_slope
+            ).astype(jnp.bfloat16)
+            g_ref[c, pl.ds(side * half, half), pl.ds(CHUNK, CHUNK)] = (
+                scaled * silu_bend * gate_tan
+            ).astype(jnp.bfloat16)
+            backward(c, side).start()
+
+    def give_back(s):
         for side in range(2):
-
-            @pl.when(places[side] > 0)
-            def _():
-                forward(c, side).wait_recv()
-
-            @pl.when(jnp.logical_and(places[side] > 0, places[side] < last))
-            def _():
-                pbuf[c, side] = pbuf[c, side] + rbuf[c, side]
-                forward(c, side).start()
-
-            @pl.when(places[side] == last)
-            def _():
-                gate_pre, up_pre, gate_tan = (
-                    pbuf[c, side, :, pl.ds(i * CHUNK, CHUNK)]
-                    + rbuf[c, side, :, pl.ds(i * CHUNK, CHUNK)]
-                    for i in range(3)
-                )
-                silu_slope, silu_bend = silu_parts(gate_pre)
-                scaled = grad[:, where].astype(jnp.float32) * up_pre
-                g_ref[c, pl.ds(side * half, half), pl.ds(0, CHUNK)] = (
-                    scaled * silu_slope
-                ).astype(jnp.bfloat16)
-                g_ref[c, pl.ds(side * half, half), pl.ds(CHUNK, CHUNK)] = (
-                    scaled * silu_bend * gate_tan
-                ).astype(jnp.bfloat16)
-                backward(c, side).start()
-
-    def give_back(c):
-        for side in range(2):
-
-            @pl.when(places[side] < last)
-            def _():
-                backward(c, side).wait_recv()
-
-            @pl.when(jnp.logical_and(places[side] > 0, places[side] < last))
-            def _():
-                backward(c, side).start()
+            c = s - (2 * last - places[side])
+            inside = jnp.logical_and(c >= 0, c < chunks)
+
+            @pl.when(inside)
+            def _(c=c, side=side):
+                give_back_side(c, side)
+
+    def give_back_side(c, side):
+        @pl.when(places[side] < last)
+        def _():
+            backward(c, side).wait_recv()
+
+        @pl.when(jnp.logical_and(places[side] > 0, places[side] < last))
+        def _():
+            backward(c, side).start()
 
     @pl.when(d == 0)
     def _():
@@ -263,22 +282,21 @@
         def _():
             multiply(s)
 
-        @pl.when(jnp.logical_and(s >= LAG, s < chunks + LAG))
-        def _():
-            relay(s - LAG)
-
-        @pl.when(s >= BACK)
-        def _():
-            give_back(s - BACK)
-
+        relay(s)
+        give_back(s)
         return carry
 
-    lax.fori_loop(0, chunks + BACK, step, 0)
+    lax.fori_loop(0, chunks + 2 * last, step, 0)
 
     def drain(c, carry):
         for side in range(2):
 
-            @pl.when(places[side] < last)
+            @pl.when(
+                jnp.logical_and(
+                    places[side] < last,
+                    jnp.logical_or(places[side] > 0, c >= chunks - FLIGHT),
+                )
+            )
             def _():
                 forward(c, side).wait_send()
 
@@ -348,11 +366,13 @@
 def update_kernel(
     colt_ref, g_ref, weight_ref, probe_ref, mean_ref, curve_ref, weight_out, mean_out, curve_out
 ):
-    sums = jnp.dot(colt_ref[...], g_ref[0], preferred_element_type=jnp.float32)
-    weight_out[...], mean_out[...], curve_out[...] = adahessian(
-        weight_ref[...], mean_ref[...], curve_ref[...],
-        sums[:, :CHUNK], probe_ref[...], sums[:, CHUNK:],
-    )
+    for k in range(GROUPED):
+        at = pl.ds(k * CHUNK, CHUNK)
+        sums = jnp.dot(colt_ref[...], g_ref[k], preferred_element_type=jnp.float32)
+        weight_out[:, at], mean_out[:, at], curve_out[:, at] = adahessian(
+            weight_ref[:, at], mean_ref[:, at], curve_ref[:, at],
+            sums[:, :CHUNK], probe_ref[:, at], sums[:, CHUNK:],
+        )
 
 
 UPDATE_ROWS = 512
@@ -361,13 +381,13 @@
 def update(colt, g, weight, probe, mean, curve):
     depth, width = weight.shape
     total = colt.shape[1]
-    block = pl.BlockSpec((UPDATE_ROWS, CHUNK), lambda i, j: (j, i))
+    block = pl.BlockSpec((UPDATE_ROWS, GROUPED * CHUNK), lambda i, j: (j, i))
     return pl.pallas_call(
         update_kernel,
-        grid=(width // CHUNK, depth // UPDATE_ROWS),
+        grid=(width // (GROUPED * CHUNK), depth // UPDATE_ROWS),
         in_specs=[
             pl.BlockSpec((UPDATE_ROWS, total), lambda i, j: (j, 0)),
-            pl.BlockSpec((1, total, 2 * CHUNK), lambda i, j: (i, 0, 0)),
+            pl.BlockSpec((GROUPED, total, 2 * CHUNK), lambda i, j: (i, 0, 0)),
             block, block, block, block,
         ],
         out_specs=(block, block, block),
@@ -386,7 +406,7 @@
     shards = lax.axis_size("dp")
     local, depth, width = tokens.shape[0], gate_weight.shape[0], gate_weight.shape[1]
     fits = shards == 4 and (shards * local) % 16 == 0 and hidden_grad.shape[0] % 16 == 0
-    if not (fits and width % CHUNK == 0 and depth % UPDATE_ROWS == 0 and width <= 2048):
+    if not (fits and width % (GROUPED * CHUNK) == 0 and depth % UPDATE_ROWS == 0 and width <= 2048):
         return plain_body(
             tokens, hidden_grad, gate_weight, up_weight, gate_probe,
             gate_mean, gate_curve, group_counts,

time: 165 us -> 110 us (0.67)
  Pallas kernels: 154 us -> 99 us
    pallas_call x1, Pallas kernels: 137 us -> 82.6 us  [exchange(): pl.pallas_call(functools.partial(exchange_kernel, shards, peers), out_sha...]
where the time goes in v3:
time: 110 us
  Pallas kernels  99 us (90%)
  local copies, waits for them, and re-layouts  8.2 us (7%)
  other arithmetic  1.72 us (2%)
    pallas_call x1, Pallas kernels, exchange(): pl.pallas_call(functools.partial(exchange_kernel, shards, peers), out_sha...  82.6 us
    pallas_call x1, Pallas kernels, update(): pl.pallas_call(update_kernel, grid=(width // (GROUPED * CHUNK), depth //...  16.4 us
    unnamed x10, local copies, waits for them, and re-layouts  6.12 us

profile of v3, /device:TPU:0, one launch (start us, length us, event | category | flops | bytes accessed | tf_op | source)
XLA Modules:
  0.0 109.6 jit_solution(15146702776282114959)
XLA Ops:
  0.6 1.2 %dynamic_slice.4 = s32[1]{0:T(128)} dynamic-slice(s32[4]{0:T(128)} %param.15, s32[]{:T(128)S(6)} %select_n.23), dynamic_slice_sizes={1} | dynamic-slice | bytes 12 | tf_op jit(solution)/shard_map/jit(dynamic_index_in_dim)/dynamic_slice | solution.py:415
  1.9 0.6 iota_compare_fusion
  2.5 1.0 broadcast_select_fusion.1.grad_ref
  3.5 0.8 tile.4
  4.4 0.1 broadcast_select_fusion.tok_ref
  4.5 0.0 copy-start
  4.5 2.0 %copy-done = bf16[1024,1792]{1,0:T(8,128)(2,1)S(1)} copy-done((bf16[1024,1792]{1,0:T(8,128)(2,1)S(1)}, bf16[1024,1792]{1,0:T(8,128)(2,1)}, u32[]{:S(2)}) %copy-start) | copy-done | bytes 3670040
  6.5 0.0 copy-start.2
  6.5 2.0 %copy-done.2 = bf16[1024,1792]{1,0:T(8,128)(2,1)S(1)} copy-done((bf16[1024,1792]{1,0:T(8,128)(2,1)S(1)}, bf16[1024,1792]{1,0:T(8,128)(2,1)}, u32[]{:S(2)}) %copy-start.2) | copy-done | bytes 3670040
  8.5 0.0 copy-start.4
  8.5 2.0 %copy-done.4 = bf16[1024,1792]{1,0:T(8,128)(2,1)S(1)} copy-done((bf16[1024,1792]{1,0:T(8,128)(2,1)S(1)}, bf16[1024,1792]{1,0:T(8,128)(2,1)}, u32[]{:S(2)}) %copy-start.4) | copy-done | bytes 3670040
  10.6 0.0 copy-start.1
  10.6 0.0 copy-start.3
  10.6 82.6 %shard_map.103 = (bf16[14,128,256]{2,1,0:T(8,128)(2,1)S(1)}, bf16[1024,128]{1,0:T(8,128)(2,1)S(1)}) custom-call(bf16[16,4096]{1,0:T(8,128)(2,1)S(1)} %broadcast_select_fusion.tok_ref, bf16[32,1792]{1,0:T(8,128)(2,1)S(1)} %broadcast_select_fusion.1.grad_ref, bf16[1024,1792]{1,0:T(8,128)(2,1)S(1)} %copy-done, bf16[1024,1792]{1,0:T(8,128)(2,1)S(1)} %copy-done.4, ...), custom_call_target="tpu_custom_call" | custom-call | tf_op jit(solution)/shard_map/pallas_call | solution.py:332
  93.2 0.0 copy-done.1
  93.2 0.0 copy-done.3
  93.2 16.4 %shard_map.104 = (bf16[1024,1792]{1,0:T(8,128)(2,1)}, f32[1024,1792]{1,0:T(8,128)}, f32[1024,1792]{1,0:T(8,128)}) custom-call(bf16[1024,128]{1,0:T(8,128)(2,1)S(1)} %get-tuple-element.5.colt_ref, bf16[14,128,256]{2,1,0:T(8,128)(2,1)S(1)} %get-tuple-element.6.g_ref, bf16[1024,1792]{1,0:T(8,128)(2,1)S(1)} %copy-done.1, bf16[1024,1792]{1,0:T(8,128)(2,1)S(1)} %copy-done.2, ...), custom_call_target="tpu_custom_call" | custom-call | tf_op jit(solution)/shard_map/pallas_call | solution.py:385
  (2 shorter events, 0.0 us)
Async XLA Ops:
  4.5 2.0 %copy-start = (bf16[1024,1792]{1,0:T(8,128)(2,1)S(1)}, bf16[1024,1792]{1,0:T(8,128)(2,1)}, u32[]{:S(2)}) copy-start(bf16[1024,1792]{1,0:T(8,128)(2,1)} %weight_ref.1) | copy-start | bytes 11010052
  6.5 2.0 %copy-start.2 = (bf16[1024,1792]{1,0:T(8,128)(2,1)S(1)}, bf16[1024,1792]{1,0:T(8,128)(2,1)}, u32[]{:S(2)}) copy-start(bf16[1024,1792]{1,0:T(8,128)(2,1)} %probe_ref.3) | copy-start | bytes 11010052
  8.5 2.0 %copy-start.4 = (bf16[1024,1792]{1,0:T(8,128)(2,1)S(1)}, bf16[1024,1792]{1,0:T(8,128)(2,1)}, u32[]{:S(2)}) copy-start(bf16[1024,1792]{1,0:T(8,128)(2,1)} %up_ref.1) | copy-start | bytes 11010052
  10.6 82.6 %copy-start.1 = (bf16[1024,1792]{1,0:T(8,128)(2,1)S(1)}, bf16[1024,1792]{1,0:T(8,128)(2,1)}, u32[]{:S(2)}) copy-start(bf16[1024,1792]{1,0:T(8,128)(2,1)} %weight_ref.1) | copy-start | bytes 11010052
  10.6 82.6 %copy-start.3 = (f32[1024,1792]{1,0:T(8,128)S(1)}, f32[1024,1792]{1,0:T(8,128)}, u32[]{:S(2)}) copy-start(f32[1024,1792]{1,0:T(8,128)} %mean_ref.1) | copy-start | bytes 22020100
